TPU v7x, 32 devices: a whole 2x2x4 slice. The times are simulated.
32 devices in a mesh: pipe: 2 (over y), dp: 4 (over z), tensor: 4 (over x, core).
Axes of the slice: x: 2, y: 2, z: 4, core: 2. Of those that a mesh axis runs over, the one named last changes fastest.
Arguments:
- tokens: bfloat16 [3072, 8192], P(('pipe', 'dp'), 'tensor'), parts along dimension 0, may hold values from -6 to 6
- pattern: int32 [128, 6], P('pipe'), parts along dimension 0, may hold values from 0 to 31, as said below
- blocks: bfloat16 [128, 6, 256, 256], P(('pipe', 'tensor'), None, 'dp'), parts along dimension 0, may hold values from -0.15625 to 0.15625
- left_factor: bfloat16 [16384, 512], P(('pipe', 'tensor'), 'dp'), parts along dimension 0, may hold values from -0.0625 to 0.0625
- right_factor: bfloat16 [1024, 16384], P(('pipe', 'dp'), 'tensor'), parts along dimension 0, may hold values from -0.25 to 0.25
- cotangent: bfloat16 [3072, 16384], P(('pipe', 'dp'), 'tensor'), parts along dimension 0, may hold values from -6 to 6
Outputs:
- hidden: bfloat16 [3072, 16384], P(('pipe', 'dp'), 'tensor'), parts along dimension 0
- token_grad: float32 [3072, 8192], P(('pipe', 'dp'), 'tensor'), parts along dimension 0
- block_grad: float32 [128, 6, 256, 256], P(('pipe', 'tensor'), None, 'dp'), parts along dimension 0
- left_grad: float32 [16384, 512], P(('pipe', 'tensor'), 'dp'), parts along dimension 0
- right_grad: float32 [1024, 16384], P(('pipe', 'dp'), 'tensor'), parts along dimension 0
There are 2 independent parts, one for each index of `pipe`. A program takes and returns all parts, laid end to end along the dimension named above; each array names one. Nothing has to cross between parts.
Inputs may be any that keep to these rules, and one draw needn't show every extreme that they name: `pattern`: row j lists the 6 input blocks feeding hidden block j: under a relabeling of the 32 input blocks drawn from the seed, they are the labels of (j mod 32) XOR s for s = 0 and then the powers of two below 32 in rising order; a row's entries are distinct.
All inputs are finite; a program needn't handle non-finite values.
Results may differ from a plain program's by a relative error of at most 0.017.
Values may be sent and summed in bfloat16 or wider, within the bound.
A program may use at most 256 MiB of HBM per device.

v0:
```python
import jax
import jax.numpy as jnp
from jax import lax
from jax.sharding import PartitionSpec as P

SQRT_HALF = 0.7071067811865476
INV_ROOT_TWO_PI = 0.3989422804014327


def gelu_parts(preact):
    normal_cdf = 0.5 * (1.0 + jax.scipy.special.erf(preact * SQRT_HALF))
    return (
        preact * normal_cdf,
        normal_cdf + preact * jnp.exp(-0.5 * preact * preact) * INV_ROOT_TWO_PI,
    )


def per_device(tokens, pattern, blocks, left_factor, right_factor, cotangent):
    tok_rows = tokens.shape[0]
    block_size = blocks.shape[3]
    local_cols = blocks.shape[0]
    slot_count = blocks.shape[1]
    full_tokens = lax.all_gather(tokens, "tensor", axis=1, tiled=True)
    block_count = full_tokens.shape[1] // block_size
    tensor_rank = lax.axis_index("tensor")
    local_pattern = lax.dynamic_slice_in_dim(pattern, tensor_rank * local_cols, local_cols, 0)
    picked = jnp.take(full_tokens.reshape(tok_rows, block_count, block_size), local_pattern, axis=1)
    inputs = picked
    butterfly = jnp.einsum(
        "tjkc,jkcd->tjd",
        inputs,
        lax.all_gather(blocks, "dp", axis=2, tiled=True),
        preferred_element_type=jnp.float32,
    )
    left_rows = lax.all_gather(left_factor, "dp", axis=1, tiled=True)
    whole_left = lax.all_gather(left_rows, "tensor", axis=0, tiled=True)
    rank_acts = jnp.dot(full_tokens, whole_left, preferred_element_type=jnp.float32).astype(
        jnp.bfloat16
    )
    inputs = rank_acts
    rank_part = jnp.dot(
        inputs,
        lax.all_gather(right_factor, "dp", axis=0, tiled=True),
        preferred_element_type=jnp.float32,
    )
    preact = butterfly.reshape(tok_rows, -1) + rank_part
    activated, slope_values = gelu_parts(preact)
    hidden = activated.astype(jnp.bfloat16)
    grad_pre = (cotangent.astype(jnp.float32) * slope_values).astype(jnp.bfloat16)
    rank_terms = lax.dot_general(
        grad_pre,
        lax.all_gather(right_factor, "dp", axis=0, tiled=True),
        (((1,), (1,)), ((), ())),
        preferred_element_type=jnp.float32,
    )
    rank_grad = lax.psum(rank_terms.astype(jnp.bfloat16), "tensor")
    right_term = lax.dot_general(
        rank_acts, grad_pre, (((0,), (0,)), ((), ())), preferred_element_type=jnp.float32
    )
    right_grad = lax.psum_scatter(
        right_term.astype(jnp.bfloat16), "dp", scatter_dimension=0, tiled=True
    ).astype(jnp.float32)
    left_term = lax.dot_general(
        tokens, rank_grad, (((0,), (0,)), ((), ())), preferred_element_type=jnp.float32
    )
    left_grad = lax.psum_scatter(
        left_term.astype(jnp.bfloat16), "dp", scatter_dimension=1, tiled=True
    ).astype(jnp.float32)
    grad_blocks = grad_pre.reshape(tok_rows, local_cols, block_size)
    block_term = jnp.einsum(
        "tjkc,tjd->jkcd", picked, grad_blocks, preferred_element_type=jnp.float32
    )
    block_grad = lax.psum_scatter(
        block_term.astype(jnp.bfloat16), "dp", scatter_dimension=2, tiled=True
    ).astype(jnp.float32)
    spread = jnp.einsum(
        "tjd,jkcd->tjkc",
        grad_blocks,
        lax.all_gather(blocks, "dp", axis=2, tiled=True),
        preferred_element_type=jnp.float32,
    )
    placed = (
        jnp.zeros((tok_rows, block_count, block_size), jnp.float32)
        .at[:, local_pattern.reshape(-1)]
        .add(spread.reshape(tok_rows, local_cols * slot_count, block_size))
    )
    token_part = lax.psum_scatter(
        placed.reshape(tok_rows, -1).astype(jnp.bfloat16), "tensor", scatter_dimension=1, tiled=True
    ).astype(jnp.float32)
    token_grad = token_part + lax.dot_general(
        rank_grad, left_rows, (((1,), (1,)), ((), ())), preferred_element_type=jnp.float32
    )
    return (hidden, token_grad, block_grad, left_grad, right_grad)


def solution(mesh):
    placed = (
        P(("pipe", "dp"), "tensor"),
        P("pipe", None),
        P(("pipe", "tensor"), None, "dp", None),
        P(("pipe", "tensor"), "dp"),
        P(("pipe", "dp"), "tensor"),
        P(("pipe", "dp"), "tensor"),
    )
    return jax.shard_map(
        per_device,
        mesh=mesh,
        in_specs=placed,
        out_specs=(
            P(("pipe", "dp"), "tensor"),
            P(("pipe", "dp"), "tensor"),
            P(("pipe", "tensor"), None, "dp", None),
            P(("pipe", "tensor"), "dp"),
            P(("pipe", "dp"), "tensor"),
        ),
        check_vma=False,
    )
```

profile of v0, /device:TPU:0, one launch (start us, length us, event | category | flops | bytes accessed | tf_op | source)
XLA Modules:
  0.0 936.8 jit_solution(5141369474184893608)
XLA Ops:
  7.2 0.0 copy-start.5
  7.2 0.0 all-gather.10.cloned.1.call-start
  7.2 0.7 all-gather.10.cloned.1.call-update
  7.9 0.0 all-gather.6.cloned.1.call-start
  8.0 2.6 copy.32
  10.5 0.0 all-gather.6.cloned.1.call-update
  10.6 0.0 all-gather.12.cloned.1.call-start
  10.6 47.9 %all-gather.10.cloned.1.call-done = bf16[2048,512]{1,0:T(8,128)(2,1)} async-done(((bf16[2048,128]{1,0:T(8,128)(2,1)}), bf16[2048,512]{1,0:T(8,128)(2,1)}) %all-gather.10.cloned.1.call-update) | async-done | bytes 2097168 | tf_op jit(solution)/shard_map/all_gather | solution.py:35
  58.5 0.0 all-gather.12.cloned.1.call-update
  58.6 0.0 all-gather.8.cloned.1.call-start
  58.6 0.5 all-gather.8.cloned.1.call-update
  59.1 0.0 all-gather.14.cloned.1.call-start
  59.2 0.5 all-gather.14.cloned.1.call-update
  59.7 0.0 all-reduce.2.cloned.1.call-start
  59.8 0.0 copy-done.5
  59.8 0.1 compare_and_fusion
  59.9 0.1 copy.31
  60.0 0.1 copy.33
  60.1 0.1 reshape.67
  60.2 45.2 %all-gather.6.cloned.1.call-done = bf16[384,8192]{0,1:T(8,128)(2,1)} async-done(((bf16[384,2048]{0,1:T(8,128)(2,1)}), bf16[384,8192]{0,1:T(8,128)(2,1)}) %all-gather.6.cloned.1.call-update) | async-done | bytes 6291472 | tf_op jit(solution)/shard_map/all_gather | solution.py:23
  105.3 8.6 copy.34
  114.0 13.0 %gather_fusion = bf16[96,384,256]{2,1,0:T(8,128)(2,1)} fusion(bf16[384,32,256]{2,0,1:T(8,128)(2,1)} %copy.34, s32[1024]{0:T(1024)S(1)} %pad_clamp_fusion), kind=kCustom, calls=%fused_computation | custom fusion | bytes 37749120 | tf_op jit(solution)/shard_map/jit(_take)/gather | solution.py:27
  126.9 24.7 %copy.35 = bf16[16,6,384,256]{2,3,1,0:T(8,128)(2,1)} copy(bf16[16,6,384,256]{3,2,1,0:T(8,128)(2,1)} %bitcast.47) | data formatting | bytes 37748736 | tf_op jit(solution)/shard_map/jit(_take)/gather | solution.py:27
  151.6 13.6 %all-gather.12.cloned.1.call-done = bf16[8192,512]{1,0:T(8,128)(2,1)} async-done(((bf16[2048,512]{1,0:T(8,128)(2,1)}), bf16[8192,512]{1,0:T(8,128)(2,1)}) %all-gather.12.cloned.1.call-update) | async-done | bytes 8388624 | tf_op jit(solution)/shard_map/all_gather | solution.py:36
  165.2 8.6 convolution_convert_fusion.3
  173.8 211.0 %all-gather.8.cloned.1.call-done = bf16[16,6,256,256]{3,2,1,0:T(8,128)(2,1)} async-done(((bf16[16,6,64,256]{3,2,1,0:T(8,128)(2,1)}), bf16[16,6,256,256]{3,2,1,0:T(8,128)(2,1)}) %all-gather.8.cloned.1.call-update) | async-done | bytes 12582928 | tf_op jit(solution)/shard_map/all_gather | solution.py:32
  384.9 16.6 %fusion.2 = f32[16,384,256,1]{1,2,3,0:T(8,128)} fusion(bf16[16,6,256,256]{3,2,1,0:T(8,128)(2,1)} %all-gather.8.cloned.1.call-done, bf16[16,6,384,256]{2,3,1,0:T(8,128)(2,1)} %copy.35, pred[16,6]{1,0:T(8,128)(4,1)S(1)} %copy.31), kind=kOutput, calls=%fused_computation.4 | convolution fusion | flops 4841275392 | bytes 37748832 | tf_op jit(solution)/shard_map/tjkc,jkcd->tjd/dot_general | solution.py:29
  401.5 6.6 copy.37
  408.1 57.2 %all-gather.14.cloned.1.call-done = bf16[512,4096]{1,0:T(8,128)(2,1)} async-done(((bf16[128,4096]{1,0:T(8,128)(2,1)}), bf16[512,4096]{1,0:T(8,128)(2,1)}) %all-gather.14.cloned.1.call-update) | async-done | bytes 4194320 | tf_op jit(solution)/shard_map/all_gather | solution.py:43
  465.3 10.5 %fusion.14 = (bf16[384,4096]{1,0:T(8,128)(2,1)S(1)}, bf16[384,4096]{1,0:T(8,128)(2,1)}) fusion(bf16[384,4096]{1,0:T(8,128)(2,1)} %param.11, f32[384,4096]{1,0:T(8,128)} %copy.37, bf16[384,512]{1,0:T(8,128)(2,1)S(1)} %convolution_convert_fusion.3, bf16[512,4096]{1,0:T(8,128)(2,1)} %all-gather.14.cloned.1.call-done), kind=kOutput, calls=%fused_computation.16 | convolution fusion | flops 1632632832 | bytes 20316160 | tf_op jit(solution)/shard_map/dot_general | solution.py:41
  475.8 0.0 copy-done.6
  475.8 2.6 convolution_convert_fusion.2
  478.5 0.0 all-reduce.2.cloned.1.call-update
  478.5 0.2 reduce-scatter.9.cloned.1.call-start
  478.7 31.1 %all-reduce.2.cloned.1.call-done = bf16[384,512]{1,0:T(8,128)(2,1)} async-done(((bf16[384,512]{1,0:T(8,128)(2,1)}), bf16[384,512]{1,0:T(8,128)(2,1)}) %all-reduce.2.cloned.1.call-update) | async-done | bytes 393232 | tf_op jit(solution)/shard_map/psum | solution.py:56
  509.8 4.1 fusion.18
  513.9 0.0 reduce-scatter.9.cloned.1.call-update
  513.9 0.0 reduce-scatter.11.cloned.1.call-start
  514.0 0.0 copy-done.2
  514.0 4.4 convolution_convert_fusion
  518.4 0.0 reduce-scatter.11.cloned.1.call-update
  518.5 0.0 reduce-scatter.5.cloned.1.call-start
  518.5 0.1 copy.38
  518.6 0.1 reshape.62
  518.7 3.3 copy.52
  522.0 0.0 copy-start
  522.0 25.2 %fusion.16 = f32[16,384,6,256]{3,1,2,0:T(8,128)} fusion(bf16[16,6,256,256]{3,2,1,0:T(8,128)(2,1)} %all-gather.8.cloned.1.call-done, bf16[384,16,256,1]{2,1,0,3:T(8,128)(2,1)S(1)} %bitcast.50), kind=kOutput, calls=%fused_computation.25 | convolution fusion | flops 4831838208 | bytes 53477376 | tf_op jit(solution)/shard_map/tjd,jkcd->tjkc/dot_general | solution.py:76
  547.2 0.0 copy-done
  547.2 5.9 broadcast_in_dim.19
  553.1 90.2 %scatter_fusion = f32[384,32,256]{2,0,1:T(8,128)} fusion(f32[384,32,256]{2,0,1:T(8,128)} %broadcast_in_dim.19, s32[96]{0:T(128)S(1)} %fusion.19, f32[96,384,256]{2,1,0:T(8,128)} %bitcast.46), kind=kCustom, calls=%fused_computation.1 | custom fusion | flops 9437184 | bytes 113246592 | tf_op jit(solution)/shard_map/scatter-add | solution.py:85
  643.3 5.4 convert_bitcast_fusion
  648.8 3.5 copy.51
  652.3 0.0 reduce-scatter.5.cloned.1.call-update
  652.3 0.3 reduce-scatter.7.cloned.1.call-start
  652.6 1.6 copy-done.1
  654.2 15.2 %fusion.6 = bf16[16,6,256,256]{3,2,1,0:T(8,128)(2,1)} fusion(bf16[16,6,384,256]{2,3,1,0:T(8,128)(2,1)} %copy.35, pred[16,6]{1,0:T(8,128)(4,1)S(1)} %copy.31, bf16[384,16,256,1]{2,1,0,3:T(8,128)(2,1)S(1)} %bitcast.51), kind=kOutput, calls=%fused_computation.10 | convolution fusion | flops 4847566848 | bytes 34603104 | tf_op jit(solution)/shard_map/tjkc,tjd->jkcd/dot_general | solution.py:70
  669.4 0.0 reduce-scatter.7.cloned.1.call-update
  669.5 0.0 reduce-scatter.9.cloned.1.call-done
  669.5 2.4 copy.42
  671.9 2.9 convert_element_type.59
  674.8 35.7 %reduce-scatter.5.cloned.1.call-done = bf16[384,2048]{1,0:T(8,128)(2,1)} async-done(((bf16[384,8192]{1,0:T(8,128)(2,1)}), bf16[384,2048]{1,0:T(8,128)(2,1)}) %reduce-scatter.5.cloned.1.call-update) | async-done | bytes 1572880 | tf_op jit(solution)/shard_map/reduce_scatter | solution.py:87
  710.4 4.1 convert_add_fusion
  714.5 210.0 %reduce-scatter.7.cloned.1.call-done = bf16[16,6,64,256]{3,2,1,0:T(8,128)(2,1)} async-done(((bf16[16,6,256,256]{3,2,1,0:T(8,128)(2,1)}), bf16[16,6,64,256]{3,2,1,0:T(8,128)(2,1)}) %reduce-scatter.7.cloned.1.call-update) | async-done | bytes 3145744 | tf_op jit(solution)/shard_map/reduce_scatter | solution.py:73
  924.5 5.5 convert_element_type.54
  (11 shorter events, 0.0 us)
Async XLA Ops:
  7.2 52.6 %copy-start.5 = (s32[64,6]{0,1:T(8,128)S(1)}, s32[64,6]{0,1:T(8,128)}, u32[]{:S(2)}) copy-start(s32[64,6]{0,1:T(8,128)} %param.7) | copy-start | bytes 4612
  7.2 51.4 %all-gather.10.cloned.1.call-start = ((), (), s32[]{:S(2)}) async-start(), calls=%async_computation.6 | async-start | bytes 2621440 | tf_op jit(solution)/shard_map/all_gather | solution.py:35
  7.9 97.4 %all-gather.6.cloned.1.call-start = ((), (), s32[]{:S(2)}) async-start(), calls=%async_computation.4 | async-start | bytes 7864320 | tf_op jit(solution)/shard_map/all_gather | solution.py:23
  10.6 154.6 %all-gather.12.cloned.1.call-start = ((), (), s32[]{:S(2)}) async-start(), calls=%async_computation.7 | async-start | bytes 10485760 | tf_op jit(solution)/shard_map/all_gather | solution.py:36
  58.6 326.3 %all-gather.8.cloned.1.call-start = ((), (), s32[]{:S(2)}) async-start(), calls=%async_computation.5 | async-start | bytes 15728640 | tf_op jit(solution)/shard_map/all_gather | solution.py:32
  59.1 406.1 %all-gather.14.cloned.1.call-start = ((), (), s32[]{:S(2)}) async-start(), calls=%async_computation.8 | async-start | bytes 5242880 | tf_op jit(solution)/shard_map/all_gather | solution.py:43
  59.7 450.0 %all-reduce.2.cloned.1.call-start = ((), (), s32[]{:S(2)}) async-start(), calls=%async_computation.10 | async-start | bytes 786432 | tf_op jit(solution)/shard_map/psum | solution.py:56
  465.3 10.5 %copy-start.6 = (bf16[512,4096]{1,0:T(8,128)(2,1)S(1)}, bf16[512,4096]{1,0:T(8,128)(2,1)}, u32[]{:S(2)}) copy-start(bf16[512,4096]{1,0:T(8,128)(2,1)} %all-gather.14.cloned.1.call-done) | copy-start | bytes 12582916
  475.8 38.2 %copy-start.2 = (bf16[384,4096]{1,0:T(8,128)(2,1)}, bf16[384,4096]{1,0:T(8,128)(2,1)S(1)}, u32[]{:S(2)}) copy-start(bf16[384,4096]{1,0:T(8,128)(2,1)S(1)} %get-tuple-element.22) | copy-start | bytes 9437188
  478.5 191.0 %reduce-scatter.9.cloned.1.call-start = ((), (), s32[]{:S(2)}) async-start(), calls=%async_computation.12 | async-start | bytes 2621440 | tf_op jit(solution)/shard_map/reduce_scatter | solution.py:66
  513.9 157.9 %reduce-scatter.11.cloned.1.call-start = ((), (), s32[]{:S(2)}) async-start(), calls=%async_computation.13 | async-start | bytes 5242880 | tf_op jit(solution)/shard_map/reduce_scatter | solution.py:60
  518.5 192.0 %reduce-scatter.5.cloned.1.call-start = ((), (), s32[]{:S(2)}) async-start(), calls=%async_computation.9 | async-start | bytes 7864320 | tf_op jit(solution)/shard_map/reduce_scatter | solution.py:87
  522.0 25.2 %copy-start = (bf16[48,8,16,256]{3,2,1,0:T(8,128)(2,1)}, bf16[48,8,16,256]{3,2,1,0:T(8,128)(2,1)S(1)}, u32[]{:S(2)}) copy-start(bf16[48,8,16,256]{3,2,1,0:T(8,128)(2,1)S(1)} %copy.52) | copy-start | bytes 9437188
  652.3 1.9 copy-start.1
  652.3 272.2 %reduce-scatter.7.cloned.1.call-start = ((), (), s32[]{:S(2)}) async-start(), calls=%async_computation.11 | async-start | bytes 15728640 | tf_op jit(solution)/shard_map/reduce_scatter | solution.py:73
  669.4 41.0 %copy-start.3 = (bf16[2048,512]{1,0:T(8,128)(2,1)S(1)}, bf16[2048,512]{1,0:T(8,128)(2,1)}, u32[]{:S(2)}) copy-start(bf16[2048,512]{1,0:T(8,128)(2,1)} %all-gather.10.cloned.1.call-done) | copy-start | bytes 6291460
  669.4 41.0 %copy-start.4 = (bf16[384,512]{1,0:T(8,128)(2,1)S(1)}, bf16[384,512]{1,0:T(8,128)(2,1)}, u32[]{:S(2)}) copy-start(bf16[384,512]{1,0:T(8,128)(2,1)} %all-reduce.2.cloned.1.call-done) | copy-start | bytes 1179652
Sparse Core Ops, SparseCore 0:
  9.6 48.9 all-gather.9
  60.7 44.5 all-gather.5
  106.9 58.2 all-gather.11
  166.6 218.2 all-gather.7
  386.3 78.9 all-gather.13
  478.6 31.1 all-reduce.1
  514.0 43.8 reduce-scatter.8
  560.2 76.0 reduce-scatter.10
  652.4 57.9 reduce-scatter.4
  712.6 211.8 reduce-scatter.6
where the time goes:
time: 939 us; the launch traced here: 937 us
  waiting for transfers between devices  654 us (70%)
  other arithmetic  104 us (11%)
  matrix products  91.5 us (10%)
  local copies, waits for them, and re-layouts  72.6 us (8%)
  between operations  14.3 us (2%)
    all_gather x1, waiting for transfers between devices, per_device(): lax.all_gather(blocks, 'dp', axis=2, tiled=True)  211 us
    reduce_scatter x1, waiting for transfers between devices, per_device(): lax.psum_scatter(block_term.astype(jnp.bfloat16), 'dp', scatter_dimension...  210 us
    scatter-add x1, other arithmetic, per_device(): placed = jnp.zeros((tok_rows, block_count, block_size), jnp.float32).at[:...  90.2 us
    all_gather x1, waiting for transfers between devices, per_device(): lax.all_gather(right_factor, 'dp', axis=0, tiled=True)  57.2 us
    all_gather x1, waiting for transfers between devices, per_device(): left_rows = lax.all_gather(left_factor, 'dp', axis=1, tiled=True)  47.9 us
    all_gather x1, waiting for transfers between devices, per_device(): full_tokens = lax.all_gather(tokens, 'tensor', axis=1, tiled=True)  45.2 us
    gather x2, local copies, waits for them, and re-layouts, per_device(): jnp.take(full_tokens.reshape(tok_rows, block_count, block_size), local_pa...  37.6 us
    reduce_scatter x1, waiting for transfers between devices, per_device(): lax.psum_scatter(placed.reshape(tok_rows, -1).astype(jnp.bfloat16), 'tens...  35.7 us
  transfers between devices with their start and end apart: 10, of which 8 were waited for; matrix products, arithmetic and copies ran while one was open for 26% of the time, Pallas kernels for 0%

commit v1 on v0

--- a/solution.py
+++ b/solution.py
@@ -5,6 +5,17 @@
 
 SQRT_HALF = 0.7071067811865476
 INV_ROOT_TWO_PI = 0.3989422804014327
+
+
+def turned_line(x, mesh_axis, dim):
+    size = lax.axis_size(mesh_axis)
+    forward = [(i, (i + 1) % size) for i in range(size)]
+    shards = [x]
+    for stride in range(1, size):
+        shards = [lax.ppermute(shards[0], mesh_axis, forward), *shards]
+    whole = jnp.concatenate(shards, axis=dim)
+    shift = (lax.axis_index(mesh_axis) + 1) * shards[-1].shape[dim]
+    return jnp.roll(whole, shift, axis=dim)
 
 
 def gelu_parts(preact):
@@ -32,7 +43,7 @@
         lax.all_gather(blocks, "dp", axis=2, tiled=True),
         preferred_element_type=jnp.float32,
     )
-    left_rows = lax.all_gather(left_factor, "dp", axis=1, tiled=True)
+    left_rows = turned_line(left_factor, "dp", 1)
     whole_left = lax.all_gather(left_rows, "tensor", axis=0, tiled=True)
     rank_acts = jnp.dot(full_tokens, whole_left, preferred_element_type=jnp.float32).astype(
         jnp.bfloat16

time: 939 us -> 893 us (0.951)
  waiting for transfers between devices: 654 us -> 601 us
    all_gather x1 -> x0, waiting for transfers between devices: 47.9 us -> none  [per_device(): left_rows = lax.all_gather(left_factor, 'dp', axis=1, tiled=True)]
    all_gather x1, waiting for transfers between devices: 45.2 us -> 0.02 us  [per_device(): full_tokens = lax.all_gather(tokens, 'tensor', axis=1, tiled=True)]
    ppermute x0 -> x3, waiting for transfers between devices: none -> 42.8 us  [turned_line(): shards = [lax.ppermute(shards[0], mesh_axis, forward), *shards]]
  transfers between devices with their start and end apart: 10 -> 12, of which waited for: 8 -> 9; matrix products, arithmetic and copies ran while one was open for 26% -> 28% of each run, Pallas kernels for 0% -> 0%
where the time goes in v1:
time: 893 us; the launch traced here: 891 us
  waiting for transfers between devices  601 us (67%)
  other arithmetic  104 us (12%)
  matrix products  92.1 us (10%)
  local copies, waits for them, and re-layouts  76 us (9%)
  between operations  14 us (2%)
    reduce_scatter x1, waiting for transfers between devices, per_device(): lax.psum_scatter(block_term.astype(jnp.bfloat16), 'dp', scatter_dimension...  210 us
    all_gather x1, waiting for transfers between devices, per_device(): lax.all_gather(blocks, 'dp', axis=2, tiled=True)  210 us
    scatter-add x1, other arithmetic, per_device(): placed = jnp.zeros((tok_rows, block_count, block_size), jnp.float32).at[:...  90.3 us
    all_gather x1, waiting for transfers between devices, per_device(): lax.all_gather(right_factor, 'dp', axis=0, tiled=True)  57.2 us
    ppermute x3, waiting for transfers between devices, turned_line(): shards = [lax.ppermute(shards[0], mesh_axis, forward), *shards]  42.8 us
    gather x2, local copies, waits for them, and re-layouts, per_device(): jnp.take(full_tokens.reshape(tok_rows, block_count, block_size), local_pa...  37.9 us
    reduce_scatter x1, waiting for transfers between devices, per_device(): lax.psum_scatter(placed.reshape(tok_rows, -1).astype(jnp.bfloat16), 'tens...  36.7 us
    psum x1, waiting for transfers between devices, per_device(): rank_grad = lax.psum(rank_terms.astype(jnp.bfloat16), 'tensor')  31 us
  transfers between devices with their start and end apart: 12, of which 9 were waited for; matrix products, arithmetic and copies ran while one was open for 28% of the time, Pallas kernels for 0%

profile of v1, /device:TPU:0, one launch (start us, length us, event | category | flops | bytes accessed | tf_op | source)
XLA Modules:
  0.0 891.3 jit_solution(4519168670593001249)
XLA Ops:
  7.2 0.0 all-gather.5.cloned.1.call-start
  7.2 2.6 copy.32
  9.9 0.0 all-gather.5.cloned.1.call-update
  9.9 0.0 all-gather.9.cloned.1.call-start
  9.9 3.1 collective-permute-start
  13.0 13.9 %collective-permute-done = bf16[2048,128]{1,0:T(8,128)(2,1)S(1)} collective-permute-done((bf16[2048,128]{1,0:T(8,128)(2,1)S(1)}, bf16[2048,128]{1,0:T(8,128)(2,1)S(1)}, u32[]{:S(2)}, u32[]{:S(2)}) %collective-permute-start) | collective-permute-done | bytes 524320 | tf_op jit(solution)/shard_map/ppermute | solution.py:15
  27.0 14.9 %collective-permute-done.1 = bf16[2048,128]{1,0:T(8,128)(2,1)S(1)} collective-permute-done((bf16[2048,128]{1,0:T(8,128)(2,1)S(1)}, bf16[2048,128]{1,0:T(8,128)(2,1)S(1)}, u32[]{:S(2)}, u32[]{:S(2)}) %collective-permute-start.1) | collective-permute-done | bytes 524320 | tf_op jit(solution)/shard_map/ppermute | solution.py:15
  41.9 14.0 %collective-permute-done.2 = bf16[2048,128]{1,0:T(8,128)(2,1)S(1)} collective-permute-done((bf16[2048,128]{1,0:T(8,128)(2,1)S(1)}, bf16[2048,128]{1,0:T(8,128)(2,1)S(1)}, u32[]{:S(2)}, u32[]{:S(2)}) %collective-permute-start.2) | collective-permute-done | bytes 524320 | tf_op jit(solution)/shard_map/ppermute | solution.py:15
  55.9 0.1 constant_dynamic-update-slice_fusion.7
  56.0 0.2 constant_dynamic-update-slice_fusion.6
  56.2 0.2 constant_dynamic-update-slice_fusion.5
  56.4 0.2 constant_dynamic-update-slice_fusion.4
  56.6 0.2 constant_dynamic-update-slice_fusion.3
  56.7 0.2 constant_dynamic-update-slice_fusion.2
  56.9 0.2 constant_dynamic-update-slice_fusion.1
  57.1 0.2 constant_dynamic-update-slice_fusion
  57.3 1.6 constant_dynamic-slice_fusion
  58.9 0.0 all-gather.9.cloned.1.call-update
  58.9 0.0 all-gather.7.cloned.1.call-start
  59.0 0.7 all-gather.7.cloned.1.call-update
  59.7 0.0 all-gather.11.cloned.1.call-start
  59.7 0.5 all-gather.11.cloned.1.call-update
  60.2 0.2 all-reduce.2.cloned.1.call-start
  60.5 0.1 compare_and_fusion
  60.6 0.1 copy.31
  60.7 0.1 copy.33
  60.8 0.1 reshape.67
  60.9 0.0 all-gather.5.cloned.1.call-done
  60.9 8.7 copy.34
  69.6 13.3 %gather_fusion = bf16[96,384,256]{2,1,0:T(8,128)(2,1)} fusion(bf16[384,32,256]{2,0,1:T(8,128)(2,1)} %copy.34, s32[1024]{0:T(1024)S(1)} %pad_clamp_fusion), kind=kCustom, calls=%fused_computation | custom fusion | bytes 37749120 | tf_op jit(solution)/shard_map/jit(_take)/gather | solution.py:38
  82.8 24.7 %copy.35 = bf16[16,6,384,256]{2,3,1,0:T(8,128)(2,1)} copy(bf16[16,6,384,256]{3,2,1,0:T(8,128)(2,1)} %bitcast.47) | data formatting | bytes 37748736 | tf_op jit(solution)/shard_map/jit(_take)/gather | solution.py:38
  107.5 11.6 %all-gather.9.cloned.1.call-done = bf16[8192,512]{1,0:T(8,128)(2,1)} async-done(((bf16[2048,512]{1,0:T(8,128)(2,1)}), bf16[8192,512]{1,0:T(8,128)(2,1)}) %all-gather.9.cloned.1.call-update) | async-done | bytes 8388624 | tf_op jit(solution)/shard_map/all_gather | solution.py:47
  119.1 9.7 %convolution_convert_fusion.3 = bf16[512,384]{1,0:T(8,128)(2,1)S(1)} fusion(bf16[8192,512]{1,0:T(8,128)(2,1)} %all-gather.9.cloned.1.call-done, bf16[384,8192]{0,1:T(8,128)(2,1)} %all-gather.5.cloned.1.call-done), kind=kOutput, calls=%fused_computation.29 | convolution fusion | flops 3221422080 | bytes 15073280 | tf_op jit(solution)/shard_map/dot_general | solution.py:48
  128.8 210.1 %all-gather.7.cloned.1.call-done = bf16[16,6,256,256]{3,2,1,0:T(8,128)(2,1)} async-done(((bf16[16,6,64,256]{3,2,1,0:T(8,128)(2,1)}), bf16[16,6,256,256]{3,2,1,0:T(8,128)(2,1)}) %all-gather.7.cloned.1.call-update) | async-done | bytes 12582928 | tf_op jit(solution)/shard_map/all_gather | solution.py:43
  339.0 16.6 %fusion.2 = f32[16,384,256,1]{1,2,3,0:T(8,128)} fusion(bf16[16,6,256,256]{3,2,1,0:T(8,128)(2,1)} %all-gather.7.cloned.1.call-done, bf16[16,6,384,256]{2,3,1,0:T(8,128)(2,1)} %copy.35, pred[16,6]{1,0:T(8,128)(4,1)S(1)} %copy.31), kind=kOutput, calls=%fused_computation.4 | convolution fusion | flops 4841275392 | bytes 37748832 | tf_op jit(solution)/shard_map/tjkc,jkcd->tjd/dot_general | solution.py:40
  355.6 6.6 copy.37
  362.2 57.2 %all-gather.11.cloned.1.call-done = bf16[512,4096]{1,0:T(8,128)(2,1)} async-done(((bf16[128,4096]{1,0:T(8,128)(2,1)}), bf16[512,4096]{1,0:T(8,128)(2,1)}) %all-gather.11.cloned.1.call-update) | async-done | bytes 4194320 | tf_op jit(solution)/shard_map/all_gather | solution.py:54
  419.4 10.5 %fusion.14 = (bf16[384,4096]{1,0:T(8,128)(2,1)S(1)}, bf16[384,4096]{1,0:T(8,128)(2,1)}) fusion(bf16[384,4096]{1,0:T(8,128)(2,1)} %param.11, f32[384,4096]{1,0:T(8,128)} %copy.37, bf16[512,384]{1,0:T(8,128)(2,1)S(1)} %convolution_convert_fusion.3, bf16[512,4096]{1,0:T(8,128)(2,1)} %all-gather.11.cloned.1.call-done), kind=kOutput, calls=%fused_computation.16 | convolution fusion | flops 1632632832 | bytes 20316160 | tf_op jit(solution)/shard_map/dot_general | solution.py:52
  429.9 2.6 convolution_convert_fusion.2
  432.5 0.0 all-reduce.2.cloned.1.call-update
  432.5 0.3 reduce-scatter.9.cloned.1.call-start
  432.8 31.0 %all-reduce.2.cloned.1.call-done = bf16[384,512]{1,0:T(8,128)(2,1)} async-done(((bf16[384,512]{1,0:T(8,128)(2,1)}), bf16[384,512]{1,0:T(8,128)(2,1)}) %all-reduce.2.cloned.1.call-update) | async-done | bytes 393232 | tf_op jit(solution)/shard_map/psum | solution.py:67
  463.8 4.1 fusion.18
  468.0 0.0 reduce-scatter.11.cloned.1.call-start
  468.0 4.4 convolution_convert_fusion
  472.5 0.0 reduce-scatter.5.cloned.1.call-start
  472.5 0.1 copy.38
  472.6 0.1 reshape.62
  472.7 3.3 copy.52
  476.0 25.3 %fusion.16 = f32[16,384,6,256]{3,1,2,0:T(8,128)} fusion(bf16[16,6,256,256]{3,2,1,0:T(8,128)(2,1)} %all-gather.7.cloned.1.call-done, bf16[384,16,256,1]{2,1,0,3:T(8,128)(2,1)S(1)} %bitcast.49), kind=kOutput, calls=%fused_computation.25 | convolution fusion | flops 4831838208 | bytes 53477376 | tf_op jit(solution)/shard_map/tjd,jkcd->tjkc/dot_general | solution.py:87
  501.3 5.9 broadcast_in_dim.19
  507.3 90.3 %scatter_fusion = f32[384,32,256]{2,0,1:T(8,128)} fusion(f32[384,32,256]{2,0,1:T(8,128)} %broadcast_in_dim.19, s32[96]{0:T(128)S(1)} %fusion.19, f32[96,384,256]{2,1,0:T(8,128)} %bitcast.46), kind=kCustom, calls=%fused_computation.1 | custom fusion | flops 9437184 | bytes 113246592 | tf_op jit(solution)/shard_map/scatter-add | solution.py:96
  597.5 5.4 convert_bitcast_fusion
  602.9 3.5 copy.51
  606.5 0.3 reduce-scatter.7.cloned.1.call-start
  606.8 1.6 copy-done.2
  608.4 14.8 %fusion.6 = bf16[16,6,256,256]{3,2,1,0:T(8,128)(2,1)} fusion(bf16[16,6,384,256]{2,3,1,0:T(8,128)(2,1)} %copy.35, pred[16,6]{1,0:T(8,128)(4,1)S(1)} %copy.31, bf16[384,16,256,1]{2,1,0,3:T(8,128)(2,1)S(1)} %bitcast.50), kind=kOutput, calls=%fused_computation.10 | convolution fusion | flops 4847566848 | bytes 34603104 | tf_op jit(solution)/shard_map/tjkc,tjd->jkcd/dot_general | solution.py:81
  623.2 0.0 reduce-scatter.9.cloned.1.call-done
  623.2 2.4 copy.42
  625.6 2.8 convert_element_type.60
  628.4 36.7 %reduce-scatter.5.cloned.1.call-done = bf16[384,2048]{1,0:T(8,128)(2,1)} async-done(((bf16[384,8192]{1,0:T(8,128)(2,1)}), bf16[384,2048]{1,0:T(8,128)(2,1)}) %reduce-scatter.5.cloned.1.call-update) | async-done | bytes 1572880 | tf_op jit(solution)/shard_map/reduce_scatter | solution.py:98
  665.1 4.1 convert_add_fusion
  669.1 210.2 %reduce-scatter.7.cloned.1.call-done = bf16[16,6,64,256]{3,2,1,0:T(8,128)(2,1)} async-done(((bf16[16,6,256,256]{3,2,1,0:T(8,128)(2,1)}), bf16[16,6,64,256]{3,2,1,0:T(8,128)(2,1)}) %reduce-scatter.7.cloned.1.call-update) | async-done | bytes 3145744 | tf_op jit(solution)/shard_map/reduce_scatter | solution.py:84
  879.3 5.5 convert_element_type.55
  (25 shorter events, 0.1 us)
Async XLA Ops:
  7.2 2.8 copy-start.4
  7.2 53.7 %all-gather.5.cloned.1.call-start = ((), (), s32[]{:S(2)}) async-start(), calls=%async_computation.4 | async-start | bytes 7864320 | tf_op jit(solution)/shard_map/all_gather | solution.py:34
  9.9 109.3 %all-gather.9.cloned.1.call-start = ((), (), s32[]{:S(2)}) async-start(), calls=%async_computation.6 | async-start | bytes 10485760 | tf_op jit(solution)/shard_map/all_gather | solution.py:47
  9.9 17.0 %collective-permute-start = (bf16[2048,128]{1,0:T(8,128)(2,1)S(1)}, bf16[2048,128]{1,0:T(8,128)(2,1)S(1)}, u32[]{:S(2)}, u32[]{:S(2)}) collective-permute-start(bf16[2048,128]{1,0:T(8,128)(2,1)S(1)} %copy-done.4), channel_id=1, source_target_pairs={{0,4},{4,8},{8,12},{12,0},{1,5},{5,9},{9,13},{13,1},{2,6},{6,10},{... | collective-permute-start | bytes 1572872 | tf_op jit(solution)/shard_map/ppermute | solution.py:15
  27.0 14.9 %collective-permute-start.1 = (bf16[2048,128]{1,0:T(8,128)(2,1)S(1)}, bf16[2048,128]{1,0:T(8,128)(2,1)S(1)}, u32[]{:S(2)}, u32[]{:S(2)}) collective-permute-start(bf16[2048,128]{1,0:T(8,128)(2,1)S(1)} %collective-permute-done), channel_id=1, source_target_pairs={{0,4},{4,8},{8,12},{12,0},{1,5},{5,9},{9,13},{13,1},{2,6},{6,10},{... | collective-permute-start | bytes 1572872 | tf_op jit(solution)/shard_map/ppermute | solution.py:15
  41.9 14.0 %collective-permute-start.2 = (bf16[2048,128]{1,0:T(8,128)(2,1)S(1)}, bf16[2048,128]{1,0:T(8,128)(2,1)S(1)}, u32[]{:S(2)}, u32[]{:S(2)}) collective-permute-start(bf16[2048,128]{1,0:T(8,128)(2,1)S(1)} %collective-permute-done.1), channel_id=1, source_target_pairs={{0,4},{4,8},{8,12},{12,0},{1,5},{5,9},{9,13},{13,1},{2,6},{6,10},{... | collective-permute-start | bytes 1572872 | tf_op jit(solution)/shard_map/ppermute | solution.py:15
  58.9 1.6 copy-start.6
  58.9 280.0 %all-gather.7.cloned.1.call-start = ((), (), s32[]{:S(2)}) async-start(), calls=%async_computation.5 | async-start | bytes 15728640 | tf_op jit(solution)/shard_map/all_gather | solution.py:43
  59.7 359.7 %all-gather.11.cloned.1.call-start = ((), (), s32[]{:S(2)}) async-start(), calls=%async_computation.7 | async-start | bytes 5242880 | tf_op jit(solution)/shard_map/all_gather | solution.py:54
  60.2 403.6 %all-reduce.2.cloned.1.call-start = ((), (), s32[]{:S(2)}) async-start(), calls=%async_computation.9 | async-start | bytes 786432 | tf_op jit(solution)/shard_map/psum | solution.py:67
  419.4 10.5 %copy-start.7 = (bf16[512,4096]{1,0:T(8,128)(2,1)S(1)}, bf16[512,4096]{1,0:T(8,128)(2,1)}, u32[]{:S(2)}) copy-start(bf16[512,4096]{1,0:T(8,128)(2,1)} %all-gather.11.cloned.1.call-done) | copy-start | bytes 12582916
  429.9 38.2 %copy-start.3 = (bf16[384,4096]{1,0:T(8,128)(2,1)}, bf16[384,4096]{1,0:T(8,128)(2,1)S(1)}, u32[]{:S(2)}) copy-start(bf16[384,4096]{1,0:T(8,128)(2,1)S(1)} %get-tuple-element.22) | copy-start | bytes 9437188
  432.5 190.7 %reduce-scatter.9.cloned.1.call-start = ((), (), s32[]{:S(2)}) async-start(), calls=%async_computation.11 | async-start | bytes 2621440 | tf_op jit(solution)/shard_map/reduce_scatter | solution.py:77
  468.0 157.6 %reduce-scatter.11.cloned.1.call-start = ((), (), s32[]{:S(2)}) async-start(), calls=%async_computation.12 | async-start | bytes 5242880 | tf_op jit(solution)/shard_map/reduce_scatter | solution.py:71
  472.5 192.6 %reduce-scatter.5.cloned.1.call-start = ((), (), s32[]{:S(2)}) async-start(), calls=%async_computation.8 | async-start | bytes 7864320 | tf_op jit(solution)/shard_map/reduce_scatter | solution.py:98
  476.0 25.3 %copy-start.1 = (bf16[48,8,16,256]{3,2,1,0:T(8,128)(2,1)}, bf16[48,8,16,256]{3,2,1,0:T(8,128)(2,1)S(1)}, u32[]{:S(2)}) copy-start(bf16[48,8,16,256]{3,2,1,0:T(8,128)(2,1)S(1)} %copy.52) | copy-start | bytes 9437188
  606.5 1.9 copy-start.2
  606.5 272.8 %reduce-scatter.7.cloned.1.call-start = ((), (), s32[]{:S(2)}) async-start(), calls=%async_computation.10 | async-start | bytes 15728640 | tf_op jit(solution)/shard_map/reduce_scatter | solution.py:84
  623.2 41.9 %copy-start = (bf16[2048,512]{1,0:T(8,128)(2,1)S(1)}, bf16[2048,512]{1,0:T(8,128)(2,1)}, u32[]{:S(2)}) copy-start(bf16[2048,512]{1,0:T(8,128)(2,1)} %constant_dynamic-slice_fusion) | copy-start | bytes 6291460
  623.2 41.9 %copy-start.5 = (bf16[384,512]{1,0:T(8,128)(2,1)S(1)}, bf16[384,512]{1,0:T(8,128)(2,1)}, u32[]{:S(2)}) copy-start(bf16[384,512]{1,0:T(8,128)(2,1)} %all-reduce.2.cloned.1.call-done) | copy-start | bytes 1179652
Sparse Core Ops, SparseCore 0:
  10.1 49.0 all-gather.4
  60.8 58.2 all-gather.8
  120.7 218.2 all-gather.6
  340.4 78.9 all-gather.10
  432.6 31.1 all-reduce.1
  468.1 43.8 reduce-scatter.8
  514.3 76.0 reduce-scatter.10
  606.6 58.3 reduce-scatter.4
  667.4 211.8 reduce-scatter.6
